TPU v7x, 32 devices: a whole 2x2x4 slice. The times are simulated.
32 devices in a mesh: section: 2 (over y), dp: 16 (over z, x, core).
Axes of the slice: x: 2, y: 2, z: 4, core: 2. Of those that a mesh axis runs over, the one named last changes fastest.
Arguments:
- acts: bfloat16 [32, 256, 768], P('dp'), may hold values from -6 to 6
- counts: int32 [32], P('dp'), may hold values from 38 to 256, as said below
- cotangent: bfloat16 [32, 256, 768], P('dp'), may hold values from -6 to 6
- norm_gains: float32 [2, 2, 768], P('section'), may hold values from 0.5 to 1.5
- w_qkv: bfloat16 [2, 768, 2304], P('section'), may hold values from -0.3125 to 0.3125
- w_out: bfloat16 [2, 768, 768], P('section'), may hold values from -0.625 to 0.625
- w_up: bfloat16 [2, 768, 3072], P('section'), may hold values from -0.21875 to 0.21875
- w_down: bfloat16 [2, 3072, 768], P('section'), may hold values from -0.109375 to 0.109375
Outputs:
- ends: float32 [2, 32, 256, 768], P('section', 'dp')
- grad_gains: float32 [2, 2, 768], P('section', None, 'dp')
- grad_qkv: float32 [2, 768, 2304], P('section', 'dp')
- grad_out: float32 [2, 768, 768], P('section', 'dp')
- grad_up: float32 [2, 768, 3072], P('section', 'dp')
- grad_down: float32 [2, 3072, 768], P('section', 'dp')
Inputs may be any that keep to these rules, and one draw needn't show every extreme that they name: In every draw one cell holds all 256 genes; the other counts are drawn independently.
All inputs are finite; a program needn't handle non-finite values.
Results may differ from a plain program's by a relative error of at most 0.03.
The roundings to bfloat16 on the way count: a program that leaves them out, or rounds other values in their place, can miss the bound.
Values may be sent and summed in bfloat16 or wider, within the bound.
A program may use at most 192 MiB of HBM per device.

v0:
```python
import jax
import jax.numpy as jnp
from jax import lax
from jax.sharding import PartitionSpec as P

HEADS = 12
HD = 64


EPSILON = 1e-05


def passed_along(block, axis, distance):
    devices = range(lax.axis_size(axis))
    route = [(i - distance, i) for i in devices if i - distance in devices]
    return lax.ppermute(block, axis, route)


def normalize(hidden, gain):
    centred = hidden - jnp.mean(hidden, axis=-1, keepdims=True)
    spread = jnp.mean(centred * centred, axis=-1, keepdims=True)
    return centred * lax.rsqrt(spread + EPSILON) * gain


def gelu_exact(values):
    return jax.nn.gelu(values, approximate=False)


def split_heads(qkv_rows):
    length = qkv_rows.shape[0]
    split_parts = qkv_rows.reshape(length, 3, HEADS, HD)
    return (split_parts[:, 0], split_parts[:, 1], split_parts[:, 2])


def masked_scores(queries, key_rows, key_valid):
    scores = jnp.einsum(
        "qhe,khe->hqk", queries, key_rows, preferred_element_type=jnp.float32
    ) * HD ** (-0.5)
    return jnp.where(key_valid[None, None, :], scores, -1e30)


def layer_forward(source, gene_count, gains, weights):
    weight_qkv, weight_out, weight_up, weight_down = weights
    length = source.shape[0]
    key_valid = jnp.arange(length) < gene_count
    normed_a = normalize(source, gains[0]).astype(jnp.bfloat16)
    qkv_rows = jnp.dot(normed_a, weight_qkv, preferred_element_type=jnp.float32).astype(
        jnp.bfloat16
    )
    queries, key_rows, value_rows = split_heads(qkv_rows)
    scores = masked_scores(queries, key_rows, key_valid)
    largest = jnp.max(scores, axis=-1, keepdims=True)
    raised = jnp.exp(scores - largest)
    summed = jnp.sum(raised, axis=-1, keepdims=True)
    log_total = largest + jnp.log(summed)
    weights_soft = (raised / summed).astype(jnp.bfloat16)
    mixed_heads = jnp.einsum(
        "hqk,khe->qhe", weights_soft, value_rows, preferred_element_type=jnp.float32
    )
    mixed_heads = mixed_heads.reshape(length, HEADS * HD).astype(jnp.bfloat16)
    mid_stream = source + jnp.dot(mixed_heads, weight_out, preferred_element_type=jnp.float32)
    normed_b = normalize(mid_stream, gains[1]).astype(jnp.bfloat16)
    up_value = jnp.dot(normed_b, weight_up, preferred_element_type=jnp.float32)
    activated = gelu_exact(up_value).astype(jnp.bfloat16)
    result = mid_stream + jnp.dot(activated, weight_down, preferred_element_type=jnp.float32)
    return (
        result,
        (normed_a, qkv_rows, log_total, mixed_heads, mid_stream, normed_b, up_value, activated),
    )


def attend_backward(qkv_rows, log_total, d_mixed, key_valid):
    length = qkv_rows.shape[0]
    queries, key_rows, value_rows = split_heads(qkv_rows)
    scores = masked_scores(queries, key_rows, key_valid)
    weights_soft = jnp.exp(scores - log_total)
    d_heads = d_mixed.reshape(length, HEADS, HD)
    d_values = jnp.einsum(
        "hqk,qhe->khe",
        weights_soft.astype(jnp.bfloat16),
        d_heads,
        preferred_element_type=jnp.float32,
    )
    d_weights = jnp.einsum("qhe,khe->hqk", d_heads, value_rows, preferred_element_type=jnp.float32)
    inner = jnp.sum(weights_soft * d_weights, axis=-1, keepdims=True)
    d_scores = (weights_soft * (d_weights - inner)).astype(jnp.bfloat16)
    d_queries = jnp.einsum(
        "hqk,khe->qhe", d_scores, key_rows, preferred_element_type=jnp.float32
    ) * HD ** (-0.5)
    d_keys = jnp.einsum(
        "hqk,qhe->khe", d_scores, queries, preferred_element_type=jnp.float32
    ) * HD ** (-0.5)
    stacked = jnp.stack([d_queries, d_keys, d_values], axis=1)
    return stacked.reshape(length, 3 * HEADS * HD).astype(jnp.bfloat16)


def backward_inputs(grad_in, source, stored, gene_count, gains, weights):
    normed_a, qkv_rows, log_total, mixed_heads, mid_stream, normed_b, up_value, activated = stored
    weight_qkv, weight_out, weight_up, weight_down = weights
    key_valid = jnp.arange(source.shape[0]) < gene_count
    d_low = grad_in.astype(jnp.bfloat16)
    d_activated = jnp.einsum("ld,fd->lf", d_low, weight_down, preferred_element_type=jnp.float32)
    unused, gelu_back = jax.vjp(gelu_exact, up_value)
    d_up = gelu_back(d_activated)[0].astype(jnp.bfloat16)
    d_normed_b = jnp.einsum("lf,df->ld", d_up, weight_up, preferred_element_type=jnp.float32)
    unused, norm_back_b = jax.vjp(normalize, mid_stream, gains[1])
    d_mid_part, d_gain_b = norm_back_b(d_normed_b)
    d_mid = grad_in + d_mid_part
    d_branch = d_mid.astype(jnp.bfloat16)
    d_mixed = jnp.einsum(
        "le,de->ld", d_branch, weight_out, preferred_element_type=jnp.float32
    ).astype(jnp.bfloat16)
    d_qkv = attend_backward(qkv_rows, log_total, d_mixed, key_valid)
    d_normed_a = jnp.einsum("le,de->ld", d_qkv, weight_qkv, preferred_element_type=jnp.float32)
    unused, norm_back_a = jax.vjp(normalize, source, gains[0])
    d_source_part, d_gain_a = norm_back_a(d_normed_a)
    d_source = d_mid + d_source_part
    return (d_source, jnp.stack([d_gain_a, d_gain_b]), (d_low, d_up, d_branch, d_qkv))


def weight_grads(stored, deltas):
    normed_a, qkv_rows, log_total, mixed_heads, mid_stream, normed_b, up_value, activated = stored
    d_low, d_up, d_branch, d_qkv = deltas
    g_qkv = jnp.einsum("ld,le->de", normed_a, d_qkv, preferred_element_type=jnp.float32)
    g_out = jnp.einsum("ld,le->de", mixed_heads, d_branch, preferred_element_type=jnp.float32)
    g_up = jnp.einsum("ld,lf->df", normed_b, d_up, preferred_element_type=jnp.float32)
    g_down = jnp.einsum("lf,ld->fd", activated, d_low, preferred_element_type=jnp.float32)
    return (g_qkv, g_out, g_up, g_down)


def add_trees(left, right):
    if left is None:
        return right
    return jax.tree.map(lambda first_part, second_part: first_part + second_part, left, right)


def body(acts, counts, cotangent, norm_gains, w_qkv, w_out, w_up, w_down):
    micro_count = acts.shape[0]
    section_index = lax.axis_index("section")
    on_first = section_index == 0
    gains = norm_gains[0]
    weights = (w_qkv[0], w_out[0], w_up[0], w_down[0])

    def cell_count(forward_tick):
        return counts[jnp.clip(forward_tick - section_index, 0, micro_count - 1)]

    arrived = jnp.zeros_like(acts[0])
    inputs, stores, results = ([], [], [])
    for forward_tick in range(micro_count + 1):
        source = jnp.where(on_first, acts[min(forward_tick, micro_count - 1)], arrived).astype(
            jnp.float32
        )
        result, stored = layer_forward(source, cell_count(forward_tick), gains, weights)
        inputs.append(source)
        stores.append(stored)
        results.append(result)
        if forward_tick < micro_count:
            arrived = passed_along(result.astype(jnp.bfloat16), "section", 1)
    returned = jnp.zeros_like(cotangent[0])
    source_grads = []
    totals = None
    for backward_tick in range(micro_count + 1):
        forward_tick = micro_count - backward_tick
        if backward_tick < micro_count:
            upstream = cotangent[micro_count - 1 - backward_tick]
        else:
            upstream = jnp.zeros_like(cotangent[0])
        grad_in = jnp.where(on_first, returned, upstream).astype(jnp.float32)
        gene_count = cell_count(forward_tick)
        stored = layer_forward(inputs[forward_tick], gene_count, gains, weights)[1]
        d_source, d_gains, deltas = backward_inputs(
            grad_in, inputs[forward_tick], stored, gene_count, gains, weights
        )
        if backward_tick < micro_count:
            returned = passed_along(d_source.astype(jnp.bfloat16), "section", -1)
        local_grads = (d_gains,) + weight_grads(stored, deltas)
        totals = add_trees(totals, local_grads)
        if backward_tick > 0:
            source_grads.append(d_source)
    shares = (
        lax.psum_scatter(totals[0], "dp", scatter_dimension=1, tiled=True),
        lax.psum_scatter(totals[1], "dp", scatter_dimension=0, tiled=True),
        lax.psum_scatter(totals[2], "dp", scatter_dimension=0, tiled=True),
        lax.psum_scatter(totals[3], "dp", scatter_dimension=0, tiled=True),
        lax.psum_scatter(totals[4], "dp", scatter_dimension=0, tiled=True),
    )
    input_grads = jnp.stack(source_grads[::-1])
    layer_outputs = jnp.stack(results[1:])
    ends = jnp.where(on_first, input_grads, layer_outputs)[None]
    grad_gains, grad_qkv, grad_out, grad_up, grad_down = shares
    return (ends, grad_gains[None], grad_qkv[None], grad_out[None], grad_up[None], grad_down[None])


def solution(mesh):
    placed = (
        P("dp", None, None),
        P("dp"),
        P("dp", None, None),
        P("section", None, None),
        P("section", None, None),
        P("section", None, None),
        P("section", None, None),
        P("section", None, None),
    )
    return jax.shard_map(
        body,
        mesh=mesh,
        in_specs=placed,
        out_specs=(
            P("section", "dp", None, None),
            P("section", None, "dp"),
            P("section", "dp", None),
            P("section", "dp", None),
            P("section", "dp", None),
            P("section", "dp", None),
        ),
        check_vma=False,
    )
```

profile of v0, /device:TPU:0, one launch (start us, length us, event | category | flops | bytes accessed | tf_op | source)
XLA Modules:
  0.0 651.8 jit_solution(8408144241964515374)
XLA Ops:
  11.8 3.2 convolution_convert_fusion.2
  15.0 2.4 copy.59
  21.0 3.6 fusion.102
  26.1 10.9 %multiply_convert_fusion.5 = (bf16[256,3072]{1,0:T(8,128)(2,1)S(1)}, f32[256,3072]{1,0:T(8,128)}, f32[256,3072]{1,0:T(8,128)}) fusion(bf16[1,768,3072]{2,1,0:T(8,128)(2,1)S(1)} %bitcast.347, f32[256,768]{1,0:T(8,128)S(1)} %get-tuple-element.44, f32[768]{0:T(1024)S(1)} %get-tuple-element.18, f32[256]{0:T(256)S(1)} %fusion.165, ...), kind=kOutput, calls=%fused_computation.89 | convolution fusion | flops 1259864064 | bytes 13374464 | tf_op jit(solution)/shard_map/dot_general | solution.py:63
  38.5 5.1 collective-permute-start
  44.8 7.0 %collective-permute-done = bf16[256,768]{1,0:T(8,128)(2,1)S(1)} collective-permute-done((bf16[256,768]{1,0:T(8,128)(2,1)S(1)}, bf16[256,768]{1,0:T(8,128)(2,1)S(1)}, u32[]{:S(2)}, u32[]{:S(2)}) %collective-permute-start) | collective-permute-done | bytes 393248 | tf_op jit(solution)/shard_map/ppermute | solution.py:16
  54.9 2.4 copy.61
  59.7 3.5 fusion.101
  64.7 10.9 %multiply_convert_fusion.4 = (bf16[256,3072]{1,0:T(8,128)(2,1)S(1)}, f32[256,3072]{1,0:T(8,128)}, f32[256,3072]{1,0:T(8,128)}) fusion(bf16[1,768,3072]{2,1,0:T(8,128)(2,1)S(1)} %bitcast.349, f32[256,768]{1,0:T(8,128)S(1)} %get-tuple-element.49, f32[256]{0:T(256)S(1)} %fusion.167, f32[256]{0:T(256)S(1)} %broadcast_multiply_fusion.2, ...), kind=kOutput, calls=%fused_computation.73 | convolution fusion | flops 1259864064 | bytes 13374464 | tf_op jit(solution)/shard_map/dot_general | solution.py:63
  75.6 2.3 fusion.199
  77.9 4.7 collective-permute-start.1
  83.7 6.0 collective-permute-done.1
  93.5 2.4 copy.63
  98.3 3.5 fusion.100
  103.4 9.6 %multiply_convert_fusion = (bf16[256,3072]{1,0:T(8,128)(2,1)}, f32[256,3072]{1,0:T(8,128)S(1)}, f32[256,3072]{1,0:T(8,128)S(1)}) fusion(bf16[1,768,3072]{2,1,0:T(8,128)(2,1)S(1)} %bitcast.351, f32[256,768]{1,0:T(8,128)S(1)} %get-tuple-element.56, f32[256]{0:T(256)S(1)} %fusion.169, f32[256]{0:T(256)S(1)} %broadcast_multiply_fusion, ...), kind=kOutput, calls=%fused_computation.45 | convolution fusion | flops 1259864064 | bytes 13374464 | tf_op jit(solution)/shard_map/dot_general | solution.py:63
  122.6 2.7 fusion.75
  135.7 8.3 %collective-permute-done.2 = bf16[256,768]{1,0:T(8,128)(2,1)S(1)} collective-permute-done((bf16[256,768]{1,0:T(8,128)(2,1)S(1)}, bf16[256,768]{1,0:T(8,128)(2,1)S(1)}, u32[]{:S(2)}, u32[]{:S(2)}) %collective-permute-start.2) | collective-permute-done | bytes 393248 | tf_op jit(solution)/shard_map/ppermute | solution.py:16
  154.0 2.7 fusion.78
  184.5 2.7 fusion.110
  196.6 4.5 add_add_fusion.3
  201.5 2.8 fusion.179
  205.9 4.3 add_add_fusion.2
  210.3 3.4 fusion.186
  215.3 6.9 %add_add_fusion.1 = f32[768,3072]{1,0:T(8,128)} fusion(f32[768,3072]{1,0:T(8,128)S(1)} %fusion.186, f32[768,3072]{1,0:T(8,128)S(1)} %fusion.185, bf16[256,3072]{1,0:T(8,128)(2,1)} %copy-done.68, f32[256,768]{1,0:T(8,128)S(1)} %copy-done.39, f32[768]{0:T(1024)S(1)} %get-tuple-element.18, f32[256]{0:T(256)S(1)} %copy-done.119, f32[256]{0:T(256)S(1)} %copy-done.103), kind=kOutput, calls=%fused_computation.1 | convolution fusion | flops 1213464576 | bytes 30675968 | tf_op jit(solution)/shard_map/ld,lf->df/dot_general | solution.py:126
  222.6 3.1 fusion.155
  227.2 5.0 add_add_fusion
  232.4 4.5 fusion.94
  239.6 13.0 %reduce-scatter.16.cloned.1.call-done = f32[48,2]{1,0:T(8,128)} async-done(((f32[768,2]{1,0:T(8,128)}), f32[48,2]{1,0:T(8,128)}) %reduce-scatter.16.cloned.1.call-update) | async-done | bytes 400
  254.0 65.5 %reduce-scatter.10.cloned.1.call-done = f32[48,768]{1,0:T(8,128)} async-done(((f32[768,768]{1,0:T(8,128)}), f32[48,768]{1,0:T(8,128)}) %reduce-scatter.10.cloned.1.call-update) | async-done | bytes 147472 | tf_op jit(solution)/shard_map/reduce_scatter | solution.py:183
  319.4 93.7 %reduce-scatter.8.cloned.1.call-done = f32[48,2304]{1,0:T(8,128)} async-done(((f32[768,2304]{1,0:T(8,128)}), f32[48,2304]{1,0:T(8,128)}) %reduce-scatter.8.cloned.1.call-update) | async-done | bytes 442384 | tf_op jit(solution)/shard_map/reduce_scatter | solution.py:182
  413.1 116.0 %reduce-scatter.12.cloned.1.call-done = f32[48,3072]{1,0:T(8,128)} async-done(((f32[768,3072]{1,0:T(8,128)}), f32[48,3072]{1,0:T(8,128)}) %reduce-scatter.12.cloned.1.call-update) | async-done | bytes 589840 | tf_op jit(solution)/shard_map/reduce_scatter | solution.py:184
  529.1 115.7 %reduce-scatter.14.cloned.1.call-done = f32[192,768]{1,0:T(8,128)} async-done(((f32[3072,768]{1,0:T(8,128)}), f32[192,768]{1,0:T(8,128)}) %reduce-scatter.14.cloned.1.call-update) | async-done | bytes 589840 | tf_op jit(solution)/shard_map/reduce_scatter | solution.py:185
  (468 shorter events, 103.1 us)
Async XLA Ops:
  7.2 245.4 %reduce-scatter.16.cloned.1.call-start = ((), (), s32[]{:S(2)}) async-start(), calls=%async_computation.9 | async-start | bytes 417792
  24.7 12.3 %slice-start.10 = ((s8[4718592]{0:T(1024)(128)(4,1)}), s8[4194304]{0:T(1024)(128)(4,1)S(1)}, s32[]{:S(2)}) async-start(s8[4718592]{0:T(1024)(128)(4,1)} %bitcast.356), calls=%async_computation.20 | async-start | bytes 8388608
  25.3 11.7 %copy-start.37 = (f32[256,768]{1,0:T(8,128)}, f32[256,768]{1,0:T(8,128)S(1)}, u32[]{:S(2)}) copy-start(f32[256,768]{1,0:T(8,128)S(1)} %get-tuple-element.44) | copy-start | bytes 2359300
  25.3 11.7 %copy-start.101 = (f32[256]{0:T(256)}, f32[256]{0:T(256)S(1)}, u32[]{:S(2)}) copy-start(f32[256]{0:T(256)S(1)} %broadcast_multiply_fusion.4) | copy-start | bytes 3076
  26.1 10.9 %copy-start.117 = (f32[256]{0:T(256)}, f32[256]{0:T(256)S(1)}, u32[]{:S(2)}) copy-start(f32[256]{0:T(256)S(1)} %fusion.165) | copy-start | bytes 3076
  26.1 10.9 %slice-start.11 = ((s8[4718592]{0:T(1024)(128)(4,1)}), s8[524288]{0:T(1024)(128)(4,1)S(1)}, s32[]{:S(2)}) async-start(s8[4718592]{0:T(1024)(128)(4,1)} %bitcast.356), calls=%async_computation.21 | async-start | bytes 1048576
  38.5 13.2 %collective-permute-start = (bf16[256,768]{1,0:T(8,128)(2,1)S(1)}, bf16[256,768]{1,0:T(8,128)(2,1)S(1)}, u32[]{:S(2)}, u32[]{:S(2)}) collective-permute-start(bf16[256,768]{1,0:T(8,128)(2,1)S(1)} %fusion.97), channel_id=1, source_target_pairs={{0,16},{1,17},{2,18},{3,19},{4,20},{5,21},{6,22},{7,23},{8,24},{9,... | collective-permute-start | bytes 1179656 | tf_op jit(solution)/shard_map/ppermute | solution.py:16
  63.2 12.3 %slice-start.12 = ((s8[4718592]{0:T(1024)(128)(4,1)}), s8[4194304]{0:T(1024)(128)(4,1)S(1)}, s32[]{:S(2)}) async-start(s8[4718592]{0:T(1024)(128)(4,1)} %bitcast.358), calls=%async_computation.22 | async-start | bytes 8388608
  63.8 11.7 %copy-start.19 = (f32[256,768]{1,0:T(8,128)}, f32[256,768]{1,0:T(8,128)S(1)}, u32[]{:S(2)}) copy-start(f32[256,768]{1,0:T(8,128)S(1)} %get-tuple-element.49) | copy-start | bytes 2359300
  63.9 11.7 %copy-start.97 = (f32[256]{0:T(256)}, f32[256]{0:T(256)S(1)}, u32[]{:S(2)}) copy-start(f32[256]{0:T(256)S(1)} %broadcast_multiply_fusion.2) | copy-start | bytes 3076
  64.6 10.9 %copy-start.109 = (f32[256]{0:T(256)}, f32[256]{0:T(256)S(1)}, u32[]{:S(2)}) copy-start(f32[256]{0:T(256)S(1)} %fusion.167) | copy-start | bytes 3076
  64.6 10.9 %slice-start.13 = ((s8[4718592]{0:T(1024)(128)(4,1)}), s8[524288]{0:T(1024)(128)(4,1)S(1)}, s32[]{:S(2)}) async-start(s8[4718592]{0:T(1024)(128)(4,1)} %bitcast.358), calls=%async_computation.23 | async-start | bytes 1048576
  75.6 14.2 %copy-start.24 = (bf16[2,256,768]{2,1,0:T(8,128)(2,1)S(1)}, bf16[2,256,768]{2,1,0:T(8,128)(2,1)}, u32[]{:S(2)}) copy-start(bf16[2,256,768]{2,1,0:T(8,128)(2,1)} %param.8) | copy-start | bytes 2359300
  77.9 11.9 %collective-permute-start.1 = (bf16[256,768]{1,0:T(8,128)(2,1)S(1)}, bf16[256,768]{1,0:T(8,128)(2,1)S(1)}, u32[]{:S(2)}, u32[]{:S(2)}) collective-permute-start(bf16[256,768]{1,0:T(8,128)(2,1)S(1)} %get-tuple-element.51), channel_id=1, source_target_pairs={{0,16},{1,17},{2,18},{3,19},{4,20},{5,21},{6,22},{7,23},{8,24},{9,... | collective-permute-start | bytes 1179656 | tf_op jit(solution)/shard_map/ppermute | solution.py:16
  102.5 10.5 %slice-start.14 = ((s8[4718592]{0:T(1024)(128)(4,1)}), s8[4194304]{0:T(1024)(128)(4,1)S(1)}, s32[]{:S(2)}) async-start(s8[4718592]{0:T(1024)(128)(4,1)} %bitcast.360), calls=%async_computation.24 | async-start | bytes 8388608
  103.1 14.2 %copy-start.22 = (f32[256,768]{1,0:T(8,128)}, f32[256,768]{1,0:T(8,128)S(1)}, u32[]{:S(2)}) copy-start(f32[256,768]{1,0:T(8,128)S(1)} %get-tuple-element.56) | copy-start | bytes 2359300
  103.1 14.2 %copy-start.100 = (f32[256]{0:T(256)}, f32[256]{0:T(256)S(1)}, u32[]{:S(2)}) copy-start(f32[256]{0:T(256)S(1)} %broadcast_multiply_fusion) | copy-start | bytes 3076
  103.4 13.9 %copy-start.112 = (f32[256]{0:T(256)}, f32[256]{0:T(256)S(1)}, u32[]{:S(2)}) copy-start(f32[256]{0:T(256)S(1)} %fusion.169) | copy-start | bytes 3076
  129.3 14.8 %slice-start.16 = ((s8[4718592]{0:T(1024)(128)(4,1)}), s8[4194304]{0:T(1024)(128)(4,1)S(1)}, s32[]{:S(2)}) async-start(s8[4718592]{0:T(1024)(128)(4,1)} %bitcast.362), calls=%async_computation.26 | async-start | bytes 8388608
  129.9 14.2 %slice-start.17 = ((s8[4718592]{0:T(1024)(128)(4,1)}), s8[524288]{0:T(1024)(128)(4,1)S(1)}, s32[]{:S(2)}) async-start(s8[4718592]{0:T(1024)(128)(4,1)} %bitcast.362), calls=%async_computation.27 | async-start | bytes 1048576
  129.9 14.2 %copy-start.144 = (f32[256,3072]{1,0:T(8,128)S(1)}, f32[256,3072]{1,0:T(8,128)}, u32[]{:S(2)}) copy-start(f32[256,3072]{1,0:T(8,128)} %get-tuple-element.50) | copy-start | bytes 9437188
  131.3 12.9 %copy-start.143 = (f32[256,3072]{1,0:T(8,128)S(1)}, f32[256,3072]{1,0:T(8,128)}, u32[]{:S(2)}) copy-start(f32[256,3072]{1,0:T(8,128)} %get-tuple-element.33) | copy-start | bytes 9437188
  131.3 15.0 %slice-start.6 = ((s8[4718592]{0:T(1024)(128)(4,1)}), s8[4194304]{0:T(1024)(128)(4,1)S(1)}, s32[]{:S(2)}) async-start(s8[4718592]{0:T(1024)(128)(4,1)} %bitcast.352), calls=%async_computation.16 | async-start | bytes 8388608
  132.7 11.3 %collective-permute-start.2 = (bf16[256,768]{1,0:T(8,128)(2,1)S(1)}, bf16[256,768]{1,0:T(8,128)(2,1)S(1)}, u32[]{:S(2)}, u32[]{:S(2)}) collective-permute-start(bf16[256,768]{1,0:T(8,128)(2,1)S(1)} %add_convert_fusion.3), channel_id=1, source_target_pairs={{16,0},{17,1},{18,2},{19,3},{20,4},{21,5},{22,6},{23,7},{24,8},{25... | collective-permute-start | bytes 1179656 | tf_op jit(solution)/shard_map/ppermute | solution.py:16
  161.3 13.5 %slice-start.18 = ((s8[4718592]{0:T(1024)(128)(4,1)}), s8[4194304]{0:T(1024)(128)(4,1)S(1)}, s32[]{:S(2)}) async-start(s8[4718592]{0:T(1024)(128)(4,1)} %bitcast.364), calls=%async_computation.28 | async-start | bytes 8388608
  163.1 11.6 %slice-start.19 = ((s8[4718592]{0:T(1024)(128)(4,1)}), s8[524288]{0:T(1024)(128)(4,1)S(1)}, s32[]{:S(2)}) async-start(s8[4718592]{0:T(1024)(128)(4,1)} %bitcast.364), calls=%async_computation.29 | async-start | bytes 1048576
  164.4 10.3 %collective-permute-start.3 = (bf16[256,768]{1,0:T(8,128)(2,1)S(1)}, bf16[256,768]{1,0:T(8,128)(2,1)S(1)}, u32[]{:S(2)}, u32[]{:S(2)}) collective-permute-start(bf16[256,768]{1,0:T(8,128)(2,1)S(1)} %get-tuple-element.24), channel_id=1, source_target_pairs={{16,0},{17,1},{18,2},{19,3},{20,4},{21,5},{22,6},{23,7},{24,8},{25... | collective-permute-start | bytes 1179656 | tf_op jit(solution)/shard_map/ppermute | solution.py:16
  166.2 10.6 %slice-start.8 = ((s8[4718592]{0:T(1024)(128)(4,1)}), s8[4194304]{0:T(1024)(128)(4,1)S(1)}, s32[]{:S(2)}) async-start(s8[4718592]{0:T(1024)(128)(4,1)} %bitcast.354), calls=%async_computation.18 | async-start | bytes 8388608
  196.6 122.8 %reduce-scatter.10.cloned.1.call-start = ((), (), s32[]{:S(2)}) async-start(), calls=%async_computation.6 | async-start | bytes 2506752 | tf_op jit(solution)/shard_map/reduce_scatter | solution.py:183
  201.2 211.9 %reduce-scatter.8.cloned.1.call-start = ((), (), s32[]{:S(2)}) async-start(), calls=%async_computation.5 | async-start | bytes 7520256 | tf_op jit(solution)/shard_map/reduce_scatter | solution.py:182
  210.2 318.9 %reduce-scatter.12.cloned.1.call-start = ((), (), s32[]{:S(2)}) async-start(), calls=%async_computation.7 | async-start | bytes 10027008 | tf_op jit(solution)/shard_map/reduce_scatter | solution.py:184
  222.2 422.6 %reduce-scatter.14.cloned.1.call-start = ((), (), s32[]{:S(2)}) async-start(), calls=%async_computation.8 | async-start | bytes 10027008 | tf_op jit(solution)/shard_map/reduce_scatter | solution.py:185
  (144 other events, 409.9 us)
Sparse Core Ops, SparseCore 0:
  196.7 55.8 reduce-scatter.15
  257.4 61.9 reduce-scatter.9
  324.0 89.0 reduce-scatter.7
  418.2 110.8 reduce-scatter.11
  533.6 111.0 reduce-scatter.13
where the time goes:
time: 659 us; the launch traced here: 652 us
  waiting for transfers between devices  427 us (65%)
  matrix products  140 us (21%)
  local copies, waits for them, and re-layouts  32.9 us (5%)
  other arithmetic  20.9 us (3%)
  between operations  16.7 us (3%)
  starting transfers between devices  14 us (2%)
    reduce_scatter x1, waiting for transfers between devices, body(): lax.psum_scatter(totals[3], 'dp', scatter_dimension=0, tiled=True)  116 us
    reduce_scatter x1, waiting for transfers between devices, body(): lax.psum_scatter(totals[4], 'dp', scatter_dimension=0, tiled=True)  116 us
    reduce_scatter x1, waiting for transfers between devices, body(): lax.psum_scatter(totals[1], 'dp', scatter_dimension=0, tiled=True)  93.7 us
    reduce_scatter x1, waiting for transfers between devices, body(): lax.psum_scatter(totals[2], 'dp', scatter_dimension=0, tiled=True)  65.5 us
    dot_general x3, matrix products, layer_forward(): up_value = jnp.dot(normed_b, weight_up, preferred_element_type=jnp.float32)  31.3 us
    ppermute x4, waiting for transfers between devices, passed_along(): return lax.ppermute(block, axis, route)  23.6 us
    unnamed x336, local copies, waits for them, and re-layouts  16.1 us
    ppermute x4, starting transfers between devices, passed_along(): return lax.ppermute(block, axis, route)  13.2 us
  transfers between devices with their start and end apart: 9, of which 9 were waited for; matrix products, arithmetic and copies ran while one was open for 8% of the time, Pallas kernels for 0%

commit v1 on v0

v1 whole, which is shorter than its diff:
```python
import functools

import jax
import jax.numpy as jnp
from jax import lax
from jax.experimental import pallas as pl
from jax.experimental.pallas import tpu as pltpu
from jax.sharding import PartitionSpec as P

HEADS = 12
HD = 64
EPSILON = 1e-05
MESH = pl.DeviceIdType.MESH
F32 = jnp.float32
BF16 = jnp.bfloat16

UNITS = 36
EARLY = 12
LAG_CORE = 2
LAG_X = 6
LAG_Z = 9
HELD = 4
VMEM_BYTES = 63 << 20


NT = (((1,), (1,)), ((), ()))
TN = (((0,), (0,)), ((), ()))


def dot(left, right):
    return jnp.dot(left, right, preferred_element_type=F32)


def dot_nt(left, right):
    return lax.dot_general(left, right, NT, preferred_element_type=F32)


def dot_tn(left, right):
    return lax.dot_general(left, right, TN, preferred_element_type=F32)


def gelu_and_slope(u):
    share = 0.5 + 0.5 * lax.erf(u * 0.5 ** 0.5)
    bell = jnp.exp(-0.5 * (u * u))
    return u * share, share + u * (bell * 0.3989422804014327)


def kernel(
    scattering, counts_ref, gains_ref, acts_ref, cotangent_ref, wq_hbm, wo_hbm, wu_hbm, wd_hbm,
    ends_ref, *rest,
):
    if scattering:
        gq_ref, go_ref, gu_ref, gd_ref, gg_ref, turned, deltas_ref, gain_ref = rest[:8]
        (core_out, keep_core, core_in, x_in, z_in, gain_held, gain_in,
         core_send, core_recv, x_send, x_recv, z_send, z_recv, gain_send, gain_recv) = rest[-15:]
        rest = rest[8:-15]
    else:
        turned, deltas_ref, gain_ref = rest[:3]
        rest = rest[3:]
    (wq, wo, wu, wd, source, upstream, relayed, a_ref, o_ref, b_ref, f_ref, probs,
     normed_1, normed_2, scale_1, scale_2, mid, wide, d_mid, d_mixed,
     weight_sem, input_sem, send_sem, recv_sem) = rest

    section = lax.axis_index("section")
    place = lax.axis_index("dp")
    partner = (1 - section, place)
    on_first = section == 0
    on_second = section == 1
    rows_in = source.shape[1]
    pairs = HEADS // 2

    z = place // 4
    x = (place // 2) % 2
    core = place % 2
    far_z = (z + 1 - 2 * (z % 2), (z + 2) % 4, 3 - z)
    core_device = (section, z * 4 + x * 2 + 1 - core)
    x_device = (section, z * 4 + (1 - x) * 2 + core)
    z_devices = [(section, other * 4 + x * 2 + core) for other in far_z]
    met = [partner] + ([core_device, x_device] + z_devices if scattering else [])

    barrier = pltpu.get_barrier_semaphore()
    for device in met:
        pl.semaphore_signal(barrier, inc=1, device_id=device, device_id_type=MESH)

    loads = [
        pltpu.make_async_copy(hbm, vmem, weight_sem.at[at])
        for at, (hbm, vmem) in enumerate(((wq_hbm, wq), (wo_hbm, wo), (wu_hbm, wu), (wd_hbm, wd)))
    ]
    acts_in = pltpu.make_async_copy(acts_ref, source, input_sem)
    cotangent_in = pltpu.make_async_copy(cotangent_ref, upstream, input_sem)

    @pl.when(on_first)
    def _():
        acts_in.start()

    for load in loads:
        load.start()

    @pl.when(on_second)
    def _():
        cotangent_in.start()

    gain_ref[...] = jnp.zeros_like(gain_ref)

    @pl.when(on_first)
    def _():
        acts_in.wait()

    @pl.when(on_second)
    def _():
        cotangent_in.wait()
        pl.semaphore_wait(barrier, len(met))

    low_lanes = lax.broadcasted_iota(jnp.int32, (rows_in, 128), 1) < HD

    def relay_copy(cell, target):
        return pltpu.make_async_remote_copy(
            src_ref=relayed.at[cell],
            dst_ref=target.at[cell],
            send_sem=send_sem.at[cell],
            recv_sem=recv_sem.at[cell],
            device_id=partner,
            device_id_type=MESH,
        )

    def place_of(share):
        return (share % 2) * 384 + ((share // 2) % 2) * 192 + (share // 4) * 48

    def turn(cell, ref, left):
        lanes = pl.ds(pl.multiple_of(cell * rows_in, 256), rows_in)
        for part in range(2):
            block = ref[:, part * 384:part * 384 + 384].T
            for at in range(8):
                start = place_of(part * 8 + at)
                turned[left, start:start + 48, lanes] = block[at * 48:at * 48 + 48]

    def turn_wide(cell):
        lanes = pl.ds(pl.multiple_of(cell * rows_in, 256), rows_in)
        for part in range(8):
            block = f_ref[:, part * 384:part * 384 + 384].T
            for at in range(8):
                start = place_of(part * 2 + at // 4)
                turned[at % 4, start:start + 48, lanes] = block[at * 48:at * 48 + 48]

    def stacked(pair_block):
        none = jnp.zeros_like(pair_block)
        return jnp.concatenate(
            [jnp.where(low_lanes, pair_block, none), jnp.where(low_lanes, none, pair_block)], axis=0
        )

    def unstacked(block):
        return jnp.where(low_lanes, block[:rows_in], block[rows_in:])

    def columns(start, width=128):
        return pl.ds(pl.multiple_of(start, 128), width)

    def norm_rows(values, row_gain, at, rows, normed, scale):
        centred = values - jnp.mean(values, axis=-1, keepdims=True)
        spread = jnp.mean(centred * centred, axis=-1, keepdims=True)
        factor = lax.rsqrt(spread + EPSILON)
        unit = centred * factor
        normed[at, rows, :] = unit
        scale[at, rows, :] = jnp.broadcast_to(factor, (values.shape[0], 128))
        return (unit * row_gain).astype(BF16)

    def norm_back(d_normed, row_gain, at, rows, normed, scale, gain_row):
        unit = normed[at, rows, :]
        product = d_normed * unit
        gain_ref[gain_row:gain_row + 1, :] += jnp.sum(product, axis=0, keepdims=True)
        e = d_normed * row_gain
        mean_e = jnp.mean(e, axis=-1, keepdims=True)
        mean_en = jnp.mean(product * row_gain, axis=-1, keepdims=True)
        return scale[at, rows, :1] * (e - mean_e - unit * mean_en)

    def whole(cell):
        return pl.ds(pl.multiple_of(cell * rows_in, 256), rows_in)

    def some(cell, part):
        return pl.ds(pl.multiple_of(cell * rows_in + part * 64, 64), 64)

    def norm_source(cell):
        for part in range(4):
            a_ref[part * 64:part * 64 + 64, :] = norm_rows(
                source[cell, pl.ds(part * 64, 64), :].astype(F32),
                gains_ref[0:1, :], cell, pl.ds(part * 64, 64), normed_1, scale_1,
            )

    def project_qkv(cell):
        a = a_ref[...]
        turn(cell, a_ref, 6)
        for tile in range(9):
            cols = slice(tile * 256, tile * 256 + 256)
            block = dot(a, wq[:, cols])
            if tile < 3:
                block = block.astype(BF16).astype(F32) * HD ** -0.5
            deltas_ref[whole(cell), tile * 256 + 4608:tile * 256 + 4864] = block.astype(BF16)

    def attention(cell):
        valid = lax.broadcasted_iota(jnp.int32, (1, rows_in), 1) < counts_ref[cell]

        def attend(pair, carry):
            start = pair * 128
            queries = stacked(deltas_ref[whole(cell), columns(start + 4608)])
            scores = dot_nt(queries, deltas_ref[whole(cell), columns(start + 5376)])
            scores = jnp.where(valid, scores, -1e30)
            raised = jnp.exp(scores - jnp.max(scores, axis=-1, keepdims=True))
            soft = raised * (1.0 / jnp.sum(raised, axis=-1, keepdims=True))
            soft = soft.astype(BF16)
            probs[cell, pair] = soft
            mixed = dot(soft, deltas_ref[whole(cell), columns(start + 6144)])
            o_ref[:, columns(start)] = unstacked(mixed).astype(BF16)
            return carry

        lax.fori_loop(0, pairs, attend, 0, unroll=True)

    def project_out(cell):
        o = o_ref[...]
        turn(cell, o_ref, 5)
        for tile in range(3):
            cols = slice(tile * 256, tile * 256 + 256)
            mid[:, cols] = source[cell, :, cols].astype(F32) + dot(o, wo[:, cols])

    def norm_mid(cell):
        for part in range(4):
            rows = pl.ds(part * 64, 64)
            b_ref[rows, :] = norm_rows(
                mid[rows, :], gains_ref[1:2, :], cell, rows, normed_2, scale_2
            )

    def go_up(cell):
        turn(cell, b_ref, 4)

        def rise(tile, carry):
            cols = columns(tile * 256, 256)
            u = dot(b_ref[...], wu[:, cols])
            value, steep = gelu_and_slope(u)
            f_ref[:, cols] = value.astype(BF16)
            deltas_ref[whole(cell), columns(tile * 256 + 768, 256)] = steep.astype(BF16)
            return carry

        lax.fori_loop(0, 12, rise, 0, unroll=True)

    def go_down(cell):
        f = f_ref[...]
        turn_wide(cell)
        for tile in range(3):
            cols = slice(tile * 256, tile * 256 + 256)
            result = mid[:, cols] + dot(f, wd[:, cols])
            ends_ref[cell, :, cols] = result
            relayed[cell, :, cols] = result.astype(BF16)

    def back_down(cell):
        deltas_ref[whole(cell), 0:768] = upstream[cell]

        def fall(tile, carry):
            start = pl.multiple_of(tile * 256, 256)
            d_active = dot_nt(upstream[cell], wd[pl.ds(start, 256), :])
            d_up = d_active * deltas_ref[whole(cell), columns(start + 768, 256)].astype(F32)
            deltas_ref[whole(cell), columns(start + 768, 256)] = d_up.astype(BF16)
            return carry

        lax.fori_loop(0, 12, fall, 0, unroll=True)

    def back_up(cell):
        d_up = deltas_ref[whole(cell), 768:3840]
        for tile in range(3):
            wide[:, tile * 256:tile * 256 + 256] = dot_nt(
                d_up, wu[tile * 256:tile * 256 + 256, :]
            )

    def norm_mid_back(cell):
        for part in range(4):
            rows = pl.ds(part * 64, 64)
            total = upstream[cell, rows, :].astype(F32) + norm_back(
                wide[rows, :], gains_ref[1:2, :], cell, rows, normed_2, scale_2, 1
            )
            d_mid[rows, :] = total
            deltas_ref[some(cell, part), 3840:4608] = total.astype(BF16)

    def back_out(cell):
        d_branch = deltas_ref[whole(cell), 3840:4608]
        for tile in range(3):
            d_mixed[:, tile * 256:tile * 256 + 256] = dot_nt(
                d_branch, wo[tile * 256:tile * 256 + 256, :]
            ).astype(BF16)

    def attention_back(cell):
        def attend_back(pair, carry):
            start = pair * 128
            queries = stacked(deltas_ref[whole(cell), columns(start + 4608)])
            key_rows = deltas_ref[whole(cell), columns(start + 5376)]
            d_out = stacked(d_mixed[:, columns(start)])
            soft = probs[cell, pair]
            d_values = dot_tn(soft, d_out)
            d_soft = dot_nt(d_out, deltas_ref[whole(cell), columns(start + 6144)])
            soft = soft.astype(F32)
            inner = jnp.sum(soft * d_soft, axis=-1, keepdims=True)
            d_scores = (soft * (d_soft - inner)).astype(BF16)
            d_queries = unstacked(dot(d_scores, key_rows)) * HD ** -0.5
            d_keys = dot_tn(d_scores, queries)
            deltas_ref[whole(cell), columns(start + 4608)] = d_queries.astype(BF16)
            deltas_ref[whole(cell), columns(start + 5376)] = d_keys.astype(BF16)
            deltas_ref[whole(cell), columns(start + 6144)] = d_values.astype(BF16)
            return carry

        lax.fori_loop(0, pairs, attend_back, 0, unroll=True)

    def back_qkv(cell):
        d_qkv = deltas_ref[whole(cell), 4608:6912]
        for tile in range(3):
            wide[:, tile * 256:tile * 256 + 256] = dot_nt(
                d_qkv, wq[tile * 256:tile * 256 + 256, :]
            )

    def norm_source_back(cell):
        for part in range(4):
            rows = pl.ds(part * 64, 64)
            total = d_mid[rows, :] + norm_back(
                wide[rows, :], gains_ref[0:1, :], cell, rows, normed_1, scale_1, 0
            )

            relayed[cell, rows, :] = total.astype(BF16)

            @pl.when(on_first)
            def _():
                ends_ref[cell, rows, :] = total

    def weights_here(t, at):
        @pl.when(t == 0)
        def _():
            loads[at].wait()

    def forward(t, cell):
        @pl.when(on_second)
        def _():
            relay_copy(cell, source).wait_recv()

        norm_source(cell)
        weights_here(t, 0)
        project_qkv(cell)
        attention(cell)
        weights_here(t, 1)
        project_out(cell)
        norm_mid(cell)
        weights_here(t, 2)
        go_up(cell)
        weights_here(t, 3)
        go_down(cell)

        @pl.when(on_first)
        def _():
            @pl.when(t == 0)
            def _():
                pl.semaphore_wait(barrier, len(met))

            relay_copy(cell, source).start()

    def nothing(at):
        del at

    def backward(cell, between=nothing):
        back_down(cell)
        between(0)
        back_up(cell)
        between(1)
        norm_mid_back(cell)
        back_out(cell)
        between(2)
        attention_back(cell)
        between(3)
        back_qkv(cell)
        norm_source_back(cell)

        @pl.when(on_second)
        def _():
            relay_copy(cell, upstream).start()

        between(4)

    def receive_gradient(cell):
        @pl.when(on_first)
        def _():
            relay_copy(cell, source).wait_send()
            relay_copy(cell, upstream).wait_recv()

        deltas_ref[whole(cell), 0:768] = upstream[cell]

    def step(t, carry):
        backwards = (1 - section) * (t // 2) + section * (t % 2)
        cell = (1 - section) * (t % 2) + section * (t // 2)

        @pl.when(backwards == 0)
        def _():
            forward(t, cell)

        @pl.when(backwards == 1)
        def _():
            receive_gradient(cell)
            backward(cell)

        return carry

    lax.fori_loop(0, 3 if scattering else 4, step, 0)

    if scattering:
        def gain_copy(at, device):
            return pltpu.make_async_remote_copy(
                src_ref=gain_held.at[min(at, 2)],
                dst_ref=gain_in.at[at],
                send_sem=gain_send.at[at],
                recv_sem=gain_recv.at[at],
                device_id=device,
                device_id_type=MESH,
            )

        def core_copy(k):
            return pltpu.make_async_remote_copy(
                src_ref=core_out.at[k % HELD], dst_ref=core_in.at[k],
                send_sem=core_send.at[k], recv_sem=core_recv.at[k],
                device_id=core_device, device_id_type=MESH,
            )

        def x_copy(k):
            rows = pl.ds(pl.multiple_of((1 - x) * 192, 16), 192)
            return pltpu.make_async_remote_copy(
                src_ref=core_in.at[k, rows], dst_ref=x_in.at[k],
                send_sem=x_send.at[k], recv_sem=x_recv.at[k],
                device_id=x_device, device_id_type=MESH,
            )

        def z_copy(k, j):
            rows = pl.ds(pl.multiple_of(far_z[j] * 48, 16), 48)
            return pltpu.make_async_remote_copy(
                src_ref=x_in.at[k, rows], dst_ref=z_in.at[k, j],
                send_sem=z_send.at[k, j], recv_sem=z_recv.at[k, j],
                device_id=z_devices[j], device_id_type=MESH,
            )

        def form(k):
            down = (k < 12).astype(jnp.int32)
            left = down * (k // 3) + (1 - down) * (
                4 + (k >= 24).astype(jnp.int32) + (k >= 27).astype(jnp.int32)
            )
            right = down * (k % 3) + (1 - down) * (k - 9)
            delta = deltas_ref[:, columns(right * 256, 256)]

            @pl.when(k >= HELD)
            def _():
                core_copy(k - HELD).wait_send()

            away = turned[left, pl.ds(pl.multiple_of((1 - core) * 384, 16), 384), :]
            core_out[k % HELD] = dot(away, delta).astype(BF16)
            core_copy(k).start()
            own = turned[left, pl.ds(pl.multiple_of(core * 384, 16), 384), :]
            keep_core[k % HELD] = dot(own, delta)

        def over_core(k):
            core_copy(k).wait_recv()
            total = keep_core[k % HELD] + core_in[k].astype(F32)
            core_in[k] = total.astype(BF16)
            x_copy(k).start()

        def over_x(k):
            x_copy(k).wait_recv()
            own = pl.ds(pl.multiple_of(x * 192, 16), 192)
            total = core_in[k, own, :].astype(F32) + x_in[k].astype(F32)
            x_in[k] = total.astype(BF16)
            for j in range(3):
                z_copy(k, j).start()

        def over_z(k):
            for j in range(3):
                z_copy(k, j).wait_recv()
            total = x_in[k, pl.ds(pl.multiple_of(z * 48, 16), 48), :].astype(F32)
            for j in range(3):
                total = total + z_in[k, j].astype(F32)

            @pl.when(k < 12)
            def _():
                rows = pl.ds(pl.multiple_of((k // 3) * 48, 8), 48)
                gd_ref[rows, columns((k % 3) * 256, 256)] = total

            @pl.when(jnp.logical_and(k >= 12, k < 24))
            def _():
                gu_ref[:, columns((k - 12) * 256, 256)] = total

            @pl.when(jnp.logical_and(k >= 24, k < 27))
            def _():
                go_ref[:, columns((k - 24) * 256, 256)] = total

            @pl.when(k >= 27)
            def _():
                gq_ref[:, columns((k - 27) * 256, 256)] = total

        receive_gradient(1)

        @pl.when(on_first)
        def _():
            def early(t, carry):
                @pl.when(t < EARLY)
                def _():
                    form(t)

                @pl.when(t >= LAG_CORE)
                def _():
                    over_core(t - LAG_CORE)

                return carry

            lax.fori_loop(0, EARLY + LAG_CORE, early, 0)

        x_turns = ((0,), (1,), (2,), (3, 4), (5,))
        z_turns = ((), (), (), (0,), (1, 2))

        def between(at):
            @pl.when(on_first)
            def _():
                for k in x_turns[at]:
                    over_x(k)
                for k in z_turns[at]:
                    over_z(k)

        backward(1, between)

        gain_held[0] = gain_ref[...]
        gain_copy(0, core_device).start()

        def later(t, carry):
            @pl.when(t < UNITS)
            def _():
                form(t)

            fresh = jnp.logical_or(on_second, t >= EARLY + LAG_CORE)

            @pl.when(jnp.logical_and(fresh, jnp.logical_and(t >= LAG_CORE, t < UNITS + LAG_CORE)))
            def _():
                over_core(t - LAG_CORE)

            @pl.when(jnp.logical_and(t >= LAG_X, t < UNITS + LAG_X))
            def _():
                over_x(t - LAG_X)

            @pl.when(t >= LAG_Z)
            def _():
                over_z(t - LAG_Z)

            @pl.when(t == 16)
            def _():
                gain_copy(0, core_device).wait()
                gain_held[1] = gain_held[0] + gain_in[0]
                gain_copy(1, x_device).start()

            @pl.when(t == 22)
            def _():
                gain_copy(1, x_device).wait()
                gain_held[2] = gain_held[1] + gain_in[1]
                for j in range(3):
                    gain_copy(2 + j, z_devices[j]).start()

            return carry

        lax.fori_loop((1 - section) * EARLY, UNITS + LAG_Z, later, 0)

        for j in range(3):
            gain_copy(2 + j, z_devices[j]).wait()
        total_gains = gain_held[2] + gain_in[2] + gain_in[3] + gain_in[4]
        chosen = (
            lax.broadcasted_iota(jnp.int32, (768, 48), 0)
            == lax.broadcasted_iota(jnp.int32, (768, 48), 1) + place * 48
        ).astype(F32)
        own_gains = jnp.dot(
            total_gains, chosen, precision=lax.Precision.HIGHEST, preferred_element_type=F32
        )
        gg_ref[...] = own_gains[:2]

        def finish(k, carry):
            @pl.when(k >= UNITS - HELD)
            def _():
                core_copy(k).wait_send()

            x_copy(k).wait_send()
            for j in range(3):
                z_copy(k, j).wait_send()
            return carry

        lax.fori_loop(0, UNITS, finish, 0)

    @pl.when(on_second)
    def _():
        for cell in range(2):
            relay_copy(cell, upstream).wait_send()


def run_kernel(scattering, acts, counts, cotangent, gains, weights):
    cells, length, width = acts.shape
    vmem = pl.BlockSpec(memory_space=pltpu.VMEM)
    anywhere = pl.BlockSpec(memory_space=pl.ANY)
    dma = pltpu.SemaphoreType.DMA
    held = (
        ((7, 768, cells * length), BF16),
        ((cells * length, 6912), BF16),
        ((8, 768), F32),
    )
    shares = (((48, 2304), F32), ((48, 768), F32), ((48, 3072), F32), ((192, 768), F32), ((2, 48), F32))
    outs = (((cells, length, width), F32),) + (shares if scattering else held)
    scratch = (held if scattering else ()) + (
        ((768, 2304), BF16),
        ((768, 768), BF16),
        ((768, 3072), BF16),
        ((3072, 768), BF16),
        ((cells, length, width), BF16),
        ((cells, length, width), BF16),
        ((cells, length, width), BF16),
        ((length, width), BF16),
        ((length, width), BF16),
        ((length, width), BF16),
        ((length, 3072), BF16),
        ((cells, HEADS // 2, 2 * length, length), BF16),
        ((cells, length, width), F32),
        ((cells, length, width), F32),
        ((cells, length, 128), F32),
        ((cells, length, 128), F32),
        ((length, width), F32),
        ((length, width), F32),
        ((length, width), F32),
        ((length, width), BF16),
    )
    semaphores = [dma((4,)), dma(()), dma((2,)), dma((2,))]
    travel = ()
    if scattering:
        travel = (
            ((HELD, 384, 256), BF16),
            ((HELD, 384, 256), F32),
            ((UNITS, 384, 256), BF16),
            ((UNITS, 192, 256), BF16),
            ((UNITS, 3, 48, 256), BF16),
            ((3, 8, 768), F32),
            ((5, 8, 768), F32),
        )
    travel_semaphores = [
        dma((UNITS,)), dma((UNITS,)), dma((UNITS,)), dma((UNITS,)),
        dma((UNITS, 3)), dma((UNITS, 3)), dma((5,)), dma((5,)),
    ] if scattering else []
    return pl.pallas_call(
        functools.partial(kernel, scattering),
        out_shape=tuple(jax.ShapeDtypeStruct(shape, kind) for shape, kind in outs),
        in_specs=[pl.BlockSpec(memory_space=pltpu.SMEM), vmem] + [anywhere] * 6,
        out_specs=(vmem,) * len(outs),
        scratch_shapes=[pltpu.VMEM(shape, kind) for shape, kind in scratch]
        + semaphores
        + [pltpu.VMEM(shape, kind) for shape, kind in travel]
        + travel_semaphores,
        compiler_params=pltpu.CompilerParams(
            collective_id=1 if scattering else 2,
            has_side_effects=True,
            vmem_limit_bytes=VMEM_BYTES,
        ),
        name="relay_layers",
    )(counts, gains, acts, cotangent, *weights)


def plain_scattered(turned, deltas, d_gains):
    d_low, d_up = deltas[:, :768], deltas[:, 768:3840]
    d_branch, d_qkv = deltas[:, 3840:4608], deltas[:, 4608:]
    rows = turned.shape[2]
    shares = turned.reshape(7, 2, 2, 4, 48, rows).transpose(3, 2, 1, 0, 4, 5).reshape(16, 7, 48, rows)
    scatter = functools.partial(lax.psum_scatter, axis_name="dp", scatter_dimension=0, tiled=True)
    return (
        lax.psum_scatter(d_gains[:2], "dp", scatter_dimension=1, tiled=True),
        scatter(dot(shares[:, 6].reshape(768, rows), d_qkv)),
        scatter(dot(shares[:, 5].reshape(768, rows), d_branch)),
        scatter(dot(shares[:, 4].reshape(768, rows), d_up)),
        scatter(dot(shares[:, :4].reshape(3072, rows), d_low)),
    )


def body(acts, counts, cotangent, norm_gains, w_qkv, w_out, w_up, w_down):
    weights = (w_qkv[0], w_out[0], w_up[0], w_down[0])
    if lax.axis_size("dp") == 16:
        ends, *shares, d_gains = run_kernel(True, acts, counts, cotangent, norm_gains[0], weights)
        shares = [d_gains] + shares
    else:
        ends, *held = run_kernel(False, acts, counts, cotangent, norm_gains[0], weights)
        shares = plain_scattered(*held)
    return (ends[None],) + tuple(share[None] for share in shares)


def solution(mesh):
    placed = (
        P("dp", None, None),
        P("dp"),
        P("dp", None, None),
        P("section", None, None),
        P("section", None, None),
        P("section", None, None),
        P("section", None, None),
        P("section", None, None),
    )
    return jax.shard_map(
        body,
        mesh=mesh,
        in_specs=placed,
        out_specs=(
            P("section", "dp", None, None),
            P("section", None, "dp"),
            P("section", "dp", None),
            P("section", "dp", None),
            P("section", "dp", None),
            P("section", "dp", None),
        ),
        check_vma=False,
    )
```

time: 659 us -> 176 us (0.27)
  waiting for transfers between devices: 427 us -> 0 us
  Pallas kernels: 0 us -> 167 us
  matrix products: 140 us -> 0 us
  local copies, waits for them, and re-layouts: 32.9 us -> 8.02 us
  other arithmetic: 20.9 us -> 0 us
  between operations: 16.7 us -> 0.67 us
  starting transfers between devices: 14 us -> 0 us
    reduce_scatter x4 -> x0, waiting for transfers between devices: 391 us -> none  [the longest x1 116 us: body(): lax.psum_scatter(totals[3], 'dp', scatter_dimension=0, tiled=True)]
    pallas_call x0 -> x1, Pallas kernels: none -> 167 us  [run_kernel(): pl.pallas_call(functools.partial(kernel, scattering), out_shape=tuple((ja...]
    dot_general x54 -> x0, matrix products: 140 us -> none  [the longest x3 31.3 us: layer_forward(): up_value = jnp.dot(normed_b, weight_up, preferred_element_type=jnp.float32)]
    ppermute x4 -> x0, waiting for transfers between devices: 23.6 us -> none  [passed_along(): return lax.ppermute(block, axis, route)]
    ppermute x4 -> x0, starting transfers between devices: 13.2 us -> none  [passed_along(): return lax.ppermute(block, axis, route)]
    unnamed x6 -> x0, waiting for transfers between devices: 13.1 us -> none
    convert_element_type x6 -> x0, local copies, waits for them, and re-layouts: 13 us -> none  [the longest x3 7.17 us: layer_forward(): jnp.dot(normed_a, weight_qkv, preferred_element_type=jnp.float32)]
    reduce_sum x18 -> x0, other arithmetic: 8.89 us -> none  [the longest x6 2.75 us: normalize(): centred = hidden - jnp.mean(hidden, axis=-1, keepdims=True)]
  transfers between devices with their start and end apart: 9 -> 0, of which waited for: 9 -> 0; matrix products, arithmetic and copies ran while one was open for 8% -> 0% of each run, Pallas kernels for 0% -> 0%
where the time goes in v1:
time: 176 us; the launch traced here: 175 us
  Pallas kernels  167 us (95%)
  local copies, waits for them, and re-layouts  8.02 us (5%)
    pallas_call x1, Pallas kernels, run_kernel(): pl.pallas_call(functools.partial(kernel, scattering), out_shape=tuple((ja...  167 us
    unnamed x12, local copies, waits for them, and re-layouts  8.02 us

profile of v1, /device:TPU:0, one launch (start us, length us, event | category | flops | bytes accessed | tf_op | source)
XLA Modules:
  0.0 175.3 jit_solution(4883387505672032482)
XLA Ops:
  0.6 166.6 %relay_layers.1 = (f32[2,256,768]{2,1,0:T(8,128)}, f32[48,2304]{1,0:T(8,128)}, f32[48,768]{1,0:T(8,128)}, f32[48,3072]{1,0:T(8,128)}, f32[192,768]{1,0:T(8,128)}, /*index=5*/f32[2,48]{1,0:T(2,128)}) custom-call(s32[2]{0:T(128)} %counts_ref.1, f32[2,768]{1,0:T(2,128)} %bitcast.20, bf16[2,256,768]{2,1,0:T(8,128)(2,1)} %acts_ref.1, ...), custom_call_target="tpu_custom_call" | custom-call | tf_op jit(solution)/shard_map/relay_layers/pallas_call | solution.py:644
  167.2 0.0 copy-start.2
  167.2 0.0 copy-start.1
  167.2 0.0 copy-start
  167.3 2.8 %copy.20 = f32[1,2,256,768]{3,2,1,0:T(8,128)} copy(f32[1,2,256,768]{3,2,1,0:T(8,128)} %bitcast.14) | data formatting | bytes 3145728
  170.0 1.2 copy.21
  171.2 1.8 %copy.22 = f32[1,48,2304]{2,1,0:T(8,128)} copy(f32[1,48,2304]{2,1,0:T(8,128)} %bitcast.18) | data formatting | bytes 884736
  173.0 0.0 copy-done.2
  173.0 0.7 copy.23
  173.6 0.0 copy-done.1
  173.6 0.8 copy.24
  174.5 0.0 copy-done
  174.5 0.8 copy.25
Async XLA Ops:
  167.2 5.8 %copy-start.2 = (f32[48,768]{1,0:T(8,128)S(1)}, f32[48,768]{1,0:T(8,128)}, u32[]{:S(2)}) copy-start(f32[48,768]{1,0:T(8,128)} %get-tuple-element.15) | copy-start | bytes 442372
  167.2 6.4 %copy-start.1 = (f32[48,3072]{1,0:T(8,128)S(1)}, f32[48,3072]{1,0:T(8,128)}, u32[]{:S(2)}) copy-start(f32[48,3072]{1,0:T(8,128)} %get-tuple-element.16) | copy-start | bytes 1769476
  167.2 7.2 %copy-start = (f32[192,768]{1,0:T(8,128)S(1)}, f32[192,768]{1,0:T(8,128)}, u32[]{:S(2)}) copy-start(f32[192,768]{1,0:T(8,128)} %get-tuple-element.17) | copy-start | bytes 1769476

commit v2 on v1

--- a/solution.py
+++ b/solution.py
@@ -15,11 +15,20 @@
 BF16 = jnp.bfloat16
 
 UNITS = 36
-EARLY = 12
+Z_FIRST = 6
+X_FIRST = UNITS - Z_FIRST
+EVERY = 5
+EARLY = 10
 LAG_CORE = 2
-LAG_X = 6
-LAG_Z = 9
-HELD = 4
+LAG_X = 4
+LAG_NEAR = 7
+LAG_FAR = 10
+LAG_Z_NEAR = 6
+LAG_Z_FAR = 9
+LAG_Z_X = 12
+HELD = 3
+SHARE_ENDS = (20, 30, 33)
+LINES = X_FIRST + 2 * Z_FIRST
 VMEM_BYTES = 63 << 20
 
 
@@ -51,15 +60,18 @@
 ):
     if scattering:
         gq_ref, go_ref, gu_ref, gd_ref, gg_ref, turned, deltas_ref, gain_ref = rest[:8]
-        (core_out, keep_core, core_in, x_in, z_in, gain_held, gain_in,
-         core_send, core_recv, x_send, x_recv, z_send, z_recv, gain_send, gain_recv) = rest[-15:]
-        rest = rest[8:-15]
+        gq_out, go_out, gu_out, gd_out, out_sem = rest[8:13]
+        (core_out, keep_core, core_in, x_in, last_in, near_in, far_in, gain_held, gain_in,
+         core_send, core_recv, x_send, x_recv, near_send, near_recv, far_send, far_recv,
+         gain_send, gain_recv) = rest[-19:]
+        rest = rest[13:-19]
     else:
         turned, deltas_ref, gain_ref = rest[:3]
         rest = rest[3:]
     (wq, wo, wu, wd, source, upstream, relayed, a_ref, o_ref, b_ref, f_ref, probs,
-     normed_1, normed_2, scale_1, scale_2, mid, wide, d_mid, d_mixed,
-     weight_sem, input_sem, send_sem, recv_sem) = rest
+     normed_1, normed_2, scale_1, scale_2, mid, wide, ends_out,
+     weight_sem, input_sem, send_sem, recv_sem, ends_sem) = rest
+    d_mid, d_mixed = mid, a_ref
 
     section = lax.axis_index("section")
     place = lax.axis_index("dp")
@@ -93,8 +105,7 @@
     def _():
         acts_in.start()
 
-    for load in loads:
-        load.start()
+    loads[0].start()
 
     @pl.when(on_second)
     def _():
@@ -122,6 +133,9 @@
             device_id=partner,
             device_id_type=MESH,
         )
+
+    def ends_copy(cell):
+        return pltpu.make_async_copy(ends_out.at[cell], ends_ref.at[cell], ends_sem.at[cell])
 
     def place_of(share):
         return (share % 2) * 384 + ((share // 2) % 2) * 192 + (share // 4) * 48
@@ -246,7 +260,7 @@
         for tile in range(3):
             cols = slice(tile * 256, tile * 256 + 256)
             result = mid[:, cols] + dot(f, wd[:, cols])
-            ends_ref[cell, :, cols] = result
+            ends_out[cell, :, cols] = result
             relayed[cell, :, cols] = result.astype(BF16)
 
     def back_down(cell):
@@ -323,7 +337,7 @@
 
             @pl.when(on_first)
             def _():
-                ends_ref[cell, rows, :] = total
+                ends_out[cell, rows, :] = total
 
     def weights_here(t, at):
         @pl.when(t == 0)
@@ -336,7 +350,13 @@
             relay_copy(cell, source).wait_recv()
 
         norm_source(cell)
-        weights_here(t, 0)
+
+        @pl.when(t == 0)
+        def _():
+            loads[0].wait()
+            for load in loads[1:]:
+                load.start()
+
         project_qkv(cell)
         attention(cell)
         weights_here(t, 1)
@@ -346,6 +366,10 @@
         go_up(cell)
         weights_here(t, 3)
         go_down(cell)
+
+        @pl.when(on_second)
+        def _():
+            ends_copy(cell).start()
 
         @pl.when(on_first)
         def _():
@@ -375,6 +399,10 @@
         def _():
             relay_copy(cell, upstream).start()
 
+        @pl.when(on_first)
+        def _():
+            ends_copy(cell).start()
+
         between(4)
 
     def receive_gradient(cell):
@@ -413,112 +441,241 @@
                 device_id_type=MESH,
             )
 
-        def core_copy(k):
+        inner = jnp.logical_or(z == 1, z == 2)
+        outer = jnp.logical_or(z == 0, z == 3)
+        near_device, far_device, mirror_device = z_devices
+        leaving = (3 - z) // 3 * 48
+        crossing = (2 - z) * 96
+        crossing_in = (2 - z) * 48
+        own_in = (z // 2) * (1 - z // 3) * 96
+
+        def block(start, count=48):
+            return pl.ds(pl.multiple_of(start, 16), count)
+
+        def z_unit(i):
+            return i * (EVERY + 1)
+
+        def x_unit(j):
+            return j + j // EVERY + 1
+
+        def core_copy(k, room):
             return pltpu.make_async_remote_copy(
-                src_ref=core_out.at[k % HELD], dst_ref=core_in.at[k],
+                src_ref=core_out.at[room], dst_ref=core_in.at[k],
                 send_sem=core_send.at[k], recv_sem=core_recv.at[k],
                 device_id=core_device, device_id_type=MESH,
             )
 
-        def x_copy(k):
-            rows = pl.ds(pl.multiple_of((1 - x) * 192, 16), 192)
+        def x_copy(j):
             return pltpu.make_async_remote_copy(
-                src_ref=core_in.at[k, rows], dst_ref=x_in.at[k],
-                send_sem=x_send.at[k], recv_sem=x_recv.at[k],
+                src_ref=core_in.at[x_unit(j), block((1 - x) * 192, 192)], dst_ref=x_in.at[j],
+                send_sem=x_send.at[j], recv_sem=x_recv.at[j],
                 device_id=x_device, device_id_type=MESH,
             )
 
-        def z_copy(k, j):
-            rows = pl.ds(pl.multiple_of(far_z[j] * 48, 16), 48)
+        def last_copy(i):
             return pltpu.make_async_remote_copy(
-                src_ref=x_in.at[k, rows], dst_ref=z_in.at[k, j],
-                send_sem=z_send.at[k, j], recv_sem=z_recv.at[k, j],
-                device_id=z_devices[j], device_id_type=MESH,
-            )
-
-        def form(k):
+                src_ref=core_in.at[z_unit(i), block((1 - x) * 192 + z * 48)], dst_ref=last_in.at[i],
+                send_sem=x_send.at[X_FIRST + i], recv_sem=x_recv.at[X_FIRST + i],
+                device_id=x_device, device_id_type=MESH,
+            )
+
+        def x_line(j):
+            return x_in.at[j], 0, j
+
+        def z_lines(i):
+            return [(core_in.at[z_unit(i)], side * 192, X_FIRST + 2 * i + side) for side in range(2)]
+
+        def near_copy(line, from_outer):
+            ref, base, slot = line
+            if from_outer:
+                source, target = ref.at[block(base + leaving, 144)], near_in.at[slot]
+            else:
+                source = ref.at[block(base + far_z[0] * 48)]
+                target = near_in.at[slot, pl.ds(0, 48)]
+            return pltpu.make_async_remote_copy(
+                src_ref=source, dst_ref=target,
+                send_sem=near_send.at[slot], recv_sem=near_recv.at[slot],
+                device_id=near_device, device_id_type=MESH,
+            )
+
+        def far_copy(line, at):
+            ref, base, slot = line
+            target, device = ((far_z[2], mirror_device), (far_z[1], far_device))[at]
+            return pltpu.make_async_remote_copy(
+                src_ref=ref.at[block(base + target * 48)], dst_ref=far_in.at[slot],
+                send_sem=far_send.at[slot, at], recv_sem=far_recv.at[slot],
+                device_id=device, device_id_type=MESH,
+            )
+
+        def start_line(line):
+            @pl.when(outer)
+            def _():
+                near_copy(line, True).start()
+
+            @pl.when(inner)
+            def _():
+                near_copy(line, False).start()
+
+        def pass_line(line):
+            @pl.when(inner)
+            def _():
+                ref, base, slot = line
+                near_copy(line, True).wait_recv()
+                rows = block(base + crossing, 96)
+                total = ref[rows, :].astype(F32) + near_in[slot, block(crossing_in, 96), :].astype(F32)
+                ref[rows, :] = total.astype(BF16)
+                far_copy(line, 0).start()
+                far_copy(line, 1).start()
+
+        def end_line(line):
+            ref, base, slot = line
+
+            @pl.when(outer)
+            def _():
+                near_copy(line, False).wait_recv()
+
+            far_copy(line, 0).wait_recv()
+            return (
+                ref[block(base + z * 48), :].astype(F32)
+                + near_in[slot, block(own_in), :].astype(F32)
+                + far_in[slot].astype(F32)
+            )
+
+        def wait_line_sends(line):
+            @pl.when(outer)
+            def _():
+                near_copy(line, True).wait_send()
+
+            @pl.when(inner)
+            def _():
+                near_copy(line, False).wait_send()
+                far_copy(line, 0).wait_send()
+                far_copy(line, 1).wait_send()
+
+        def form(k, room):
             down = (k < 12).astype(jnp.int32)
             left = down * (k // 3) + (1 - down) * (
                 4 + (k >= 24).astype(jnp.int32) + (k >= 27).astype(jnp.int32)
             )
             right = down * (k % 3) + (1 - down) * (k - 9)
             delta = deltas_ref[:, columns(right * 256, 256)]
-
-            @pl.when(k >= HELD)
-            def _():
-                core_copy(k - HELD).wait_send()
-
-            away = turned[left, pl.ds(pl.multiple_of((1 - core) * 384, 16), 384), :]
-            core_out[k % HELD] = dot(away, delta).astype(BF16)
-            core_copy(k).start()
-            own = turned[left, pl.ds(pl.multiple_of(core * 384, 16), 384), :]
-            keep_core[k % HELD] = dot(own, delta)
-
-        def over_core(k):
-            core_copy(k).wait_recv()
-            total = keep_core[k % HELD] + core_in[k].astype(F32)
-            core_in[k] = total.astype(BF16)
-            x_copy(k).start()
-
-        def over_x(k):
-            x_copy(k).wait_recv()
-            own = pl.ds(pl.multiple_of(x * 192, 16), 192)
-            total = core_in[k, own, :].astype(F32) + x_in[k].astype(F32)
-            x_in[k] = total.astype(BF16)
-            for j in range(3):
-                z_copy(k, j).start()
-
-        def over_z(k):
-            for j in range(3):
-                z_copy(k, j).wait_recv()
-            total = x_in[k, pl.ds(pl.multiple_of(z * 48, 16), 48), :].astype(F32)
-            for j in range(3):
-                total = total + z_in[k, j].astype(F32)
-
+            away = turned[left, block((1 - core) * 384, 384), :]
+            core_out[room] = dot(away, delta).astype(BF16)
+            core_copy(k, room).start()
+            own = turned[left, block(core * 384, 384), :]
+            keep_core[room] = dot(own, delta)
+
+        def form_z(i):
+            @pl.when(i >= 1)
+            def _():
+                core_copy(z_unit(i - 1), HELD).wait_send()
+
+            form(z_unit(i), HELD)
+
+        def form_x(j):
+            @pl.when(j >= HELD)
+            def _():
+                core_copy(x_unit(j - HELD), j % HELD).wait_send()
+
+            form(x_unit(j), j % HELD)
+
+        def over_core(k, room):
+            core_copy(k, room).wait_recv()
+            core_in[k] = (keep_core[room] + core_in[k].astype(F32)).astype(BF16)
+
+        def over_core_z(i):
+            over_core(z_unit(i), HELD)
+            for line in z_lines(i):
+                start_line(line)
+
+        def over_core_x(j):
+            over_core(x_unit(j), j % HELD)
+            x_copy(j).start()
+
+        def over_x(j):
+            x_copy(j).wait_recv()
+            own = core_in[x_unit(j), block(x * 192, 192), :].astype(F32)
+            x_in[j] = (own + x_in[j].astype(F32)).astype(BF16)
+            start_line(x_line(j))
+
+        def pass_z(i):
+            for line in z_lines(i):
+                pass_line(line)
+
+        def end_z(i):
+            for ref, base, slot in z_lines(i):
+                ref[block(base + z * 48), :] = end_line((ref, base, slot)).astype(BF16)
+            last_copy(i).start()
+
+        def store(k, total):
             @pl.when(k < 12)
             def _():
                 rows = pl.ds(pl.multiple_of((k // 3) * 48, 8), 48)
-                gd_ref[rows, columns((k % 3) * 256, 256)] = total
+                gd_out[rows, columns((k % 3) * 256, 256)] = total
 
             @pl.when(jnp.logical_and(k >= 12, k < 24))
             def _():
-                gu_ref[:, columns((k - 12) * 256, 256)] = total
+                gu_out[:, columns((k - 12) * 256, 256)] = total
 
             @pl.when(jnp.logical_and(k >= 24, k < 27))
             def _():
-                go_ref[:, columns((k - 24) * 256, 256)] = total
+                go_out[:, columns((k - 24) * 256, 256)] = total
 
             @pl.when(k >= 27)
             def _():
-                gq_ref[:, columns((k - 27) * 256, 256)] = total
+                gq_out[:, columns((k - 27) * 256, 256)] = total
+
+        def over_last(i):
+            last_copy(i).wait_recv()
+            own = core_in[z_unit(i), block(x * 192 + z * 48), :].astype(F32)
+            store(z_unit(i), own + last_in[i].astype(F32))
+
+        def end_x(j):
+            store(x_unit(j), end_line(x_line(j)))
+
+        share_copies = [
+            pltpu.make_async_copy(vmem, hbm, out_sem.at[at])
+            for at, (vmem, hbm) in enumerate(
+                ((gd_out, gd_ref), (gu_out, gu_ref), (go_out, go_ref), (gq_out, gq_ref))
+            )
+        ]
 
         receive_gradient(1)
 
         @pl.when(on_first)
         def _():
             def early(t, carry):
+                @pl.when(jnp.logical_and(t < EARLY, t % EVERY == 0))
+                def _():
+                    form_z(t // EVERY)
+
                 @pl.when(t < EARLY)
                 def _():
-                    form(t)
+                    form_x(t)
+
+                @pl.when(jnp.logical_and(t >= LAG_CORE, t % EVERY == LAG_CORE))
+                def _():
+                    over_core_z(t // EVERY)
 
                 @pl.when(t >= LAG_CORE)
                 def _():
-                    over_core(t - LAG_CORE)
+                    over_core_x(t - LAG_CORE)
 
                 return carry
 
             lax.fori_loop(0, EARLY + LAG_CORE, early, 0)
-
-        x_turns = ((0,), (1,), (2,), (3, 4), (5,))
-        z_turns = ((), (), (), (0,), (1, 2))
 
         def between(at):
             @pl.when(on_first)
             def _():
-                for k in x_turns[at]:
-                    over_x(k)
-                for k in z_turns[at]:
-                    over_z(k)
+                for j in ((0, 1, 2), (3,), (4,), (5,), ())[at]:
+                    over_x(j)
+                if at == 1:
+                    pass_z(0)
+                for j in ((), (), (0,), (1,), (2,))[at]:
+                    pass_line(x_line(j))
+                if at == 3:
+                    end_z(0)
 
         backward(1, between)
 
@@ -526,23 +683,36 @@
         gain_copy(0, core_device).start()
 
         def later(t, carry):
-            @pl.when(t < UNITS)
-            def _():
-                form(t)
-
-            fresh = jnp.logical_or(on_second, t >= EARLY + LAG_CORE)
-
-            @pl.when(jnp.logical_and(fresh, jnp.logical_and(t >= LAG_CORE, t < UNITS + LAG_CORE)))
-            def _():
-                over_core(t - LAG_CORE)
-
-            @pl.when(jnp.logical_and(t >= LAG_X, t < UNITS + LAG_X))
-            def _():
-                over_x(t - LAG_X)
-
-            @pl.when(t >= LAG_Z)
-            def _():
-                over_z(t - LAG_Z)
+            def at(lag, low, high, work):
+                @pl.when(jnp.logical_and(t >= lag + low, t < lag + high))
+                def _():
+                    work(t - lag)
+
+            def at_z(lag, work):
+                @pl.when(jnp.logical_and(
+                    (t - lag) % EVERY == 0, jnp.logical_and(t >= lag, t < lag + X_FIRST)
+                ))
+                def _():
+                    work((t - lag) // EVERY)
+
+            at_z(0, form_z)
+            at(0, 0, X_FIRST, form_x)
+
+            @pl.when(jnp.logical_or(on_second, t >= EARLY + LAG_CORE))
+            def _():
+                at_z(LAG_CORE, over_core_z)
+                at(LAG_CORE, 0, X_FIRST, over_core_x)
+
+            at(LAG_X, 0, X_FIRST, over_x)
+            at_z(LAG_Z_NEAR, pass_z)
+            at(LAG_NEAR, 0, X_FIRST, lambda j: pass_line(x_line(j)))
+            at_z(LAG_Z_FAR, end_z)
+            at_z(LAG_Z_X, over_last)
+            at(LAG_FAR, 0, X_FIRST, end_x)
+            for copy, last in zip(share_copies, SHARE_ENDS):
+                @pl.when(t == last)
+                def _():
+                    copy.start()
 
             @pl.when(t == 16)
             def _():
@@ -559,7 +729,8 @@
 
             return carry
 
-        lax.fori_loop((1 - section) * EARLY, UNITS + LAG_Z, later, 0)
+        lax.fori_loop((1 - section) * EARLY, X_FIRST + LAG_FAR, later, 0)
+        share_copies[3].start()
 
         for j in range(3):
             gain_copy(2 + j, z_devices[j]).wait()
@@ -573,17 +744,29 @@
         )
         gg_ref[...] = own_gains[:2]
 
-        def finish(k, carry):
-            @pl.when(k >= UNITS - HELD)
-            def _():
-                core_copy(k).wait_send()
-
-            x_copy(k).wait_send()
-            for j in range(3):
-                z_copy(k, j).wait_send()
+        def finish_x(j, carry):
+            @pl.when(j >= X_FIRST - HELD)
+            def _():
+                core_copy(x_unit(j), j % HELD).wait_send()
+
+            x_copy(j).wait_send()
+            wait_line_sends(x_line(j))
             return carry
 
-        lax.fori_loop(0, UNITS, finish, 0)
+        def finish_z(i, carry):
+            for line in z_lines(i):
+                wait_line_sends(line)
+            last_copy(i).wait_send()
+            return carry
+
+        core_copy(z_unit(Z_FIRST - 1), HELD).wait_send()
+        lax.fori_loop(0, X_FIRST, finish_x, 0)
+        lax.fori_loop(0, Z_FIRST, finish_z, 0)
+        for copy in share_copies:
+            copy.wait()
+
+    for cell in range(2):
+        ends_copy(cell).wait()
 
     @pl.when(on_second)
     def _():
@@ -603,7 +786,8 @@
     )
     shares = (((48, 2304), F32), ((48, 768), F32), ((48, 3072), F32), ((192, 768), F32), ((2, 48), F32))
     outs = (((cells, length, width), F32),) + (shares if scattering else held)
-    scratch = (held if scattering else ()) + (
+    first = [pltpu.VMEM(shape, kind) for shape, kind in held + shares[:4]] + [dma((4,))]
+    scratch = (
         ((768, 2304), BF16),
         ((768, 768), BF16),
         ((768, 3072), BF16),
@@ -622,31 +806,34 @@
         ((cells, length, 128), F32),
         ((length, width), F32),
         ((length, width), F32),
-        ((length, width), F32),
-        ((length, width), BF16),
+        ((cells, length, width), F32),
     )
-    semaphores = [dma((4,)), dma(()), dma((2,)), dma((2,))]
+    semaphores = [dma((4,)), dma(()), dma((2,)), dma((2,)), dma((2,))]
     travel = ()
     if scattering:
         travel = (
-            ((HELD, 384, 256), BF16),
-            ((HELD, 384, 256), F32),
+            ((HELD + 1, 384, 256), BF16),
+            ((HELD + 1, 384, 256), F32),
             ((UNITS, 384, 256), BF16),
-            ((UNITS, 192, 256), BF16),
-            ((UNITS, 3, 48, 256), BF16),
+            ((X_FIRST, 192, 256), BF16),
+            ((Z_FIRST, 48, 256), BF16),
+            ((LINES, 144, 256), BF16),
+            ((LINES, 48, 256), BF16),
             ((3, 8, 768), F32),
             ((5, 8, 768), F32),
         )
     travel_semaphores = [
         dma((UNITS,)), dma((UNITS,)), dma((UNITS,)), dma((UNITS,)),
-        dma((UNITS, 3)), dma((UNITS, 3)), dma((5,)), dma((5,)),
+        dma((LINES,)), dma((LINES,)), dma((LINES, 2)), dma((LINES,)),
+        dma((5,)), dma((5,)),
     ] if scattering else []
     return pl.pallas_call(
         functools.partial(kernel, scattering),
         out_shape=tuple(jax.ShapeDtypeStruct(shape, kind) for shape, kind in outs),
         in_specs=[pl.BlockSpec(memory_space=pltpu.SMEM), vmem] + [anywhere] * 6,
-        out_specs=(vmem,) * len(outs),
-        scratch_shapes=[pltpu.VMEM(shape, kind) for shape, kind in scratch]
+        out_specs=(anywhere,) + ((anywhere,) * 4 + (vmem,) if scattering else (vmem,) * 3),
+        scratch_shapes=(first if scattering else [])
+        + [pltpu.VMEM(shape, kind) for shape, kind in scratch]
         + semaphores
         + [pltpu.VMEM(shape, kind) for shape, kind in travel]
         + travel_semaphores,
@@ -657,6 +844,43 @@
         ),
         name="relay_layers",
     )(counts, gains, acts, cotangent, *weights)
+
+
+def hand_over_kernel(*refs):
+    count = (len(refs) - 2) // 3
+    sources, targets, rooms = (refs[at * count:(at + 1) * count] for at in range(3))
+    read_sem, write_sem = refs[-2:]
+    pieces = []
+    for source, target, room in zip(sources, targets, rooms):
+        if len(source.shape) == 3:
+            for cell in range(source.shape[0]):
+                pieces.append((source.at[cell], room.at[cell], target.at[cell]))
+        else:
+            pieces.append((source, room, target))
+    reads, writes = [], []
+    for at, (source, room, target) in enumerate(pieces):
+        reads.append(pltpu.make_async_copy(source, room, read_sem.at[at]))
+        writes.append(pltpu.make_async_copy(room, target, write_sem.at[at]))
+    for read in reads:
+        read.start()
+    for read, write in zip(reads, writes):
+        read.wait()
+        write.start()
+    for write in writes:
+        write.wait()
+
+
+def hand_over(*arrays):
+    anywhere = pl.BlockSpec(memory_space=pl.ANY)
+    sem = pltpu.SemaphoreType.DMA((len(arrays) + 1,))
+    return pl.pallas_call(
+        hand_over_kernel,
+        out_shape=tuple(jax.ShapeDtypeStruct(array.shape, array.dtype) for array in arrays),
+        in_specs=[anywhere] * len(arrays),
+        out_specs=(anywhere,) * len(arrays),
+        scratch_shapes=[pltpu.VMEM(array.shape, array.dtype) for array in arrays] + [sem, sem],
+        name="hand_over",
+    )(*arrays)
 
 
 def plain_scattered(turned, deltas, d_gains):
@@ -677,7 +901,9 @@
 def body(acts, counts, cotangent, norm_gains, w_qkv, w_out, w_up, w_down):
     weights = (w_qkv[0], w_out[0], w_up[0], w_down[0])
     if lax.axis_size("dp") == 16:
-        ends, *shares, d_gains = run_kernel(True, acts, counts, cotangent, norm_gains[0], weights)
+        ends, *shares, d_gains = hand_over(
+            *run_kernel(True, acts, counts, cotangent, norm_gains[0], weights)
+        )
         shares = [d_gains] + shares
     else:
         ends, *held = run_kernel(False, acts, counts, cotangent, norm_gains[0], weights)

time: 176 us -> 158 us (0.90)
  Pallas kernels: 167 us -> 157 us
  local copies, waits for them, and re-layouts: 8.02 us -> 0 us
    pallas_call x1, Pallas kernels: 167 us -> 154 us  [run_kernel(): pl.pallas_call(functools.partial(kernel, scattering), out_shape=tuple((ja...]
    unnamed x12 -> x0, local copies, waits for them, and re-layouts: 8.02 us -> none
    pallas_call x0 -> x1, Pallas kernels: none -> 2.98 us  [hand_over(): pl.pallas_call(hand_over_kernel, out_shape=tuple((jax.ShapeDtypeStruct(ar...]
where the time goes in v2:
time: 158 us; the launch traced here: 157 us
  Pallas kernels  157 us (99%)
    pallas_call x1, Pallas kernels, run_kernel(): pl.pallas_call(functools.partial(kernel, scattering), out_shape=tuple((ja...  154 us

profile of v2, /device:TPU:0, one launch (start us, length us, event | category | flops | bytes accessed | tf_op | source)
XLA Modules:
  0.0 157.5 jit_solution(644209659681027846)
XLA Ops:
  0.6 153.7 %relay_layers.1 = (f32[2,256,768]{2,1,0:T(8,128)}, f32[48,2304]{1,0:T(8,128)}, f32[48,768]{1,0:T(8,128)}, f32[48,3072]{1,0:T(8,128)}, f32[192,768]{1,0:T(8,128)}, /*index=5*/f32[2,48]{1,0:T(2,128)}) custom-call(s32[2]{0:T(128)} %counts_ref.1, f32[2,768]{1,0:T(2,128)} %bitcast.15, bf16[2,256,768]{2,1,0:T(8,128)(2,1)} %acts_ref.1, ...), custom_call_target="tpu_custom_call" | custom-call | tf_op jit(solution)/shard_map/relay_layers/pallas_call | solution.py:830
  154.4 3.0 %hand_over.1 = (f32[2,256,768]{2,1,0:T(8,128)}, f32[48,2304]{1,0:T(8,128)}, f32[48,768]{1,0:T(8,128)}, f32[48,3072]{1,0:T(8,128)}, f32[192,768]{1,0:T(8,128)}, /*index=5*/f32[2,48]{1,0:T(2,128)}) custom-call(f32[2,256,768]{2,1,0:T(8,128)} %get-tuple-element.18.refs_0_, f32[48,2304]{1,0:T(8,128)} %get-tuple-element.19.refs_1_, ...), custom_call_target="tpu_custom_call" | custom-call | tf_op jit(solution)/shard_map/hand_over/pallas_call | solution.py:876

commit v3 on v2

--- a/solution.py
+++ b/solution.py
@@ -21,11 +21,12 @@
 EARLY = 10
 LAG_CORE = 2
 LAG_X = 4
-LAG_NEAR = 7
+LAG_NEAR = 6
 LAG_FAR = 10
 LAG_Z_NEAR = 6
 LAG_Z_FAR = 9
 LAG_Z_X = 12
+LAG_SENT = 14
 HELD = 3
 SHARE_ENDS = (20, 30, 33)
 LINES = X_FIRST + 2 * Z_FIRST
@@ -252,7 +253,7 @@
             deltas_ref[whole(cell), columns(tile * 256 + 768, 256)] = steep.astype(BF16)
             return carry
 
-        lax.fori_loop(0, 12, rise, 0, unroll=True)
+        lax.fori_loop(0, 12, rise, 0, unroll=6)
 
     def go_down(cell):
         f = f_ref[...]
@@ -273,7 +274,7 @@
             deltas_ref[whole(cell), columns(start + 768, 256)] = d_up.astype(BF16)
             return carry
 
-        lax.fori_loop(0, 12, fall, 0, unroll=True)
+        lax.fori_loop(0, 12, fall, 0, unroll=6)
 
     def back_up(cell):
         d_up = deltas_ref[whole(cell), 768:3840]
@@ -633,6 +634,15 @@
         def end_x(j):
             store(x_unit(j), end_line(x_line(j)))
 
+        def sent_x(j):
+            x_copy(j).wait_send()
+            wait_line_sends(x_line(j))
+
+        def sent_z(i):
+            for line in z_lines(i):
+                wait_line_sends(line)
+            last_copy(i).wait_send()
+
         share_copies = [
             pltpu.make_async_copy(vmem, hbm, out_sem.at[at])
             for at, (vmem, hbm) in enumerate(
@@ -672,7 +682,7 @@
                     over_x(j)
                 if at == 1:
                     pass_z(0)
-                for j in ((), (), (0,), (1,), (2,))[at]:
+                for j in ((), (0,), (1,), (2,), (3,))[at]:
                     pass_line(x_line(j))
                 if at == 3:
                     end_z(0)
@@ -709,6 +719,8 @@
             at_z(LAG_Z_FAR, end_z)
             at_z(LAG_Z_X, over_last)
             at(LAG_FAR, 0, X_FIRST, end_x)
+            at(LAG_SENT, 0, X_FIRST, sent_x)
+            at_z(LAG_SENT, sent_z)
             for copy, last in zip(share_copies, SHARE_ENDS):
                 @pl.when(t == last)
                 def _():
@@ -727,41 +739,32 @@
                 for j in range(3):
                     gain_copy(2 + j, z_devices[j]).start()
 
+            @pl.when(t == 28)
+            def _():
+                for j in range(3):
+                    gain_copy(2 + j, z_devices[j]).wait()
+                total_gains = gain_held[2] + gain_in[2] + gain_in[3] + gain_in[4]
+                chosen = (
+                    lax.broadcasted_iota(jnp.int32, (768, 48), 0)
+                    == lax.broadcasted_iota(jnp.int32, (768, 48), 1) + place * 48
+                ).astype(F32)
+                own_gains = jnp.dot(
+                    total_gains, chosen, precision=lax.Precision.HIGHEST, preferred_element_type=F32
+                )
+                gg_ref[...] = own_gains[:2]
+
             return carry
 
         lax.fori_loop((1 - section) * EARLY, X_FIRST + LAG_FAR, later, 0)
         share_copies[3].start()
 
-        for j in range(3):
-            gain_copy(2 + j, z_devices[j]).wait()
-        total_gains = gain_held[2] + gain_in[2] + gain_in[3] + gain_in[4]
-        chosen = (
-            lax.broadcasted_iota(jnp.int32, (768, 48), 0)
-            == lax.broadcasted_iota(jnp.int32, (768, 48), 1) + place * 48
-        ).astype(F32)
-        own_gains = jnp.dot(
-            total_gains, chosen, precision=lax.Precision.HIGHEST, preferred_element_type=F32
-        )
-        gg_ref[...] = own_gains[:2]
-
-        def finish_x(j, carry):
-            @pl.when(j >= X_FIRST - HELD)
-            def _():
-                core_copy(x_unit(j), j % HELD).wait_send()
-
-            x_copy(j).wait_send()
-            wait_line_sends(x_line(j))
-            return carry
-
-        def finish_z(i, carry):
-            for line in z_lines(i):
-                wait_line_sends(line)
-            last_copy(i).wait_send()
-            return carry
-
         core_copy(z_unit(Z_FIRST - 1), HELD).wait_send()
-        lax.fori_loop(0, X_FIRST, finish_x, 0)
-        lax.fori_loop(0, Z_FIRST, finish_z, 0)
+        for j in range(X_FIRST - HELD, X_FIRST):
+            core_copy(x_unit(j), j % HELD).wait_send()
+        for j in range(X_FIRST + LAG_FAR - LAG_SENT, X_FIRST):
+            sent_x(j)
+        for i in range((X_FIRST + LAG_FAR - 1 - LAG_SENT) // EVERY + 1, Z_FIRST):
+            sent_z(i)
         for copy in share_copies:
             copy.wait()
 

time: 158 us -> 157 us (level)
  no operation moved by 1% of the time
where the time goes in v3:
time: 157 us
  Pallas kernels  156 us (99%)
    pallas_call x1, Pallas kernels, run_kernel(): pl.pallas_call(functools.partial(kernel, scattering), out_shape=tuple((ja...  153 us

profile of v3, /device:TPU:0, one launch (start us, length us, event | category | flops | bytes accessed | tf_op | source)
XLA Modules:
  0.0 156.9 jit_solution(4285176802653861389)
XLA Ops:
  0.6 153.1 %relay_layers.1 = (f32[2,256,768]{2,1,0:T(8,128)}, f32[48,2304]{1,0:T(8,128)}, f32[48,768]{1,0:T(8,128)}, f32[48,3072]{1,0:T(8,128)}, f32[192,768]{1,0:T(8,128)}, /*index=5*/f32[2,48]{1,0:T(2,128)}) custom-call(s32[2]{0:T(128)} %counts_ref.1, f32[2,768]{1,0:T(2,128)} %bitcast.15, bf16[2,256,768]{2,1,0:T(8,128)(2,1)} %acts_ref.1, ...), custom_call_target="tpu_custom_call" | custom-call | tf_op jit(solution)/shard_map/relay_layers/pallas_call | solution.py:833
  153.7 3.0 %hand_over.1 = (f32[2,256,768]{2,1,0:T(8,128)}, f32[48,2304]{1,0:T(8,128)}, f32[48,768]{1,0:T(8,128)}, f32[48,3072]{1,0:T(8,128)}, f32[192,768]{1,0:T(8,128)}, /*index=5*/f32[2,48]{1,0:T(2,128)}) custom-call(f32[2,256,768]{2,1,0:T(8,128)} %get-tuple-element.18.refs_0_, f32[48,2304]{1,0:T(8,128)} %get-tuple-element.19.refs_1_, ...), custom_call_target="tpu_custom_call" | custom-call | tf_op jit(solution)/shard_map/hand_over/pallas_call | solution.py:879

commit v4 on v3

--- a/solution.py
+++ b/solution.py
@@ -856,8 +856,11 @@
     pieces = []
     for source, target, room in zip(sources, targets, rooms):
         if len(source.shape) == 3:
+            half = source.shape[1] // 2
             for cell in range(source.shape[0]):
-                pieces.append((source.at[cell], room.at[cell], target.at[cell]))
+                for side in range(2):
+                    rows = pl.ds(side * half, half)
+                    pieces.append(tuple(ref.at[cell, rows] for ref in (source, room, target)))
         else:
             pieces.append((source, room, target))
     reads, writes = [], []
@@ -875,7 +878,7 @@
 
 def hand_over(*arrays):
     anywhere = pl.BlockSpec(memory_space=pl.ANY)
-    sem = pltpu.SemaphoreType.DMA((len(arrays) + 1,))
+    sem = pltpu.SemaphoreType.DMA((len(arrays) + 3,))
     return pl.pallas_call(
         hand_over_kernel,
         out_shape=tuple(jax.ShapeDtypeStruct(array.shape, array.dtype) for array in arrays),

time: 157 us -> 157 us (level)
  no operation moved by 1% of the time
where the time goes in v4:
time: 157 us
  Pallas kernels  156 us (99%)
    pallas_call x1, Pallas kernels, run_kernel(): pl.pallas_call(functools.partial(kernel, scattering), out_shape=tuple((ja...  153 us

profile of v4, /device:TPU:0, one launch (start us, length us, event | category | flops | bytes accessed | tf_op | source)
XLA Modules:
  0.0 156.8 jit_solution(11740233956163725543)
XLA Ops:
  0.6 153.1 %relay_layers.1 = (f32[2,256,768]{2,1,0:T(8,128)}, f32[48,2304]{1,0:T(8,128)}, f32[48,768]{1,0:T(8,128)}, f32[48,3072]{1,0:T(8,128)}, f32[192,768]{1,0:T(8,128)}, /*index=5*/f32[2,48]{1,0:T(2,128)}) custom-call(s32[2]{0:T(128)} %counts_ref.1, f32[2,768]{1,0:T(2,128)} %bitcast.15, bf16[2,256,768]{2,1,0:T(8,128)(2,1)} %acts_ref.1, ...), custom_call_target="tpu_custom_call" | custom-call | tf_op jit(solution)/shard_map/relay_layers/pallas_call | solution.py:833
  153.7 2.9 %hand_over.1 = (f32[2,256,768]{2,1,0:T(8,128)}, f32[48,2304]{1,0:T(8,128)}, f32[48,768]{1,0:T(8,128)}, f32[48,3072]{1,0:T(8,128)}, f32[192,768]{1,0:T(8,128)}, /*index=5*/f32[2,48]{1,0:T(2,128)}) custom-call(f32[2,256,768]{2,1,0:T(8,128)} %get-tuple-element.18.refs_0_, f32[48,2304]{1,0:T(8,128)} %get-tuple-element.19.refs_1_, ...), custom_call_target="tpu_custom_call" | custom-call | tf_op jit(solution)/shard_map/hand_over/pallas_call | solution.py:882

commit v5 on v3

--- a/solution.py
+++ b/solution.py
@@ -678,11 +678,11 @@
         def between(at):
             @pl.when(on_first)
             def _():
-                for j in ((0, 1, 2), (3,), (4,), (5,), ())[at]:
+                for j in ((0,), (1, 2), (3,), (4,), (5,))[at]:
                     over_x(j)
                 if at == 1:
                     pass_z(0)
-                for j in ((), (0,), (1,), (2,), (3,))[at]:
+                for j in ((), (), (0,), (1, 2), (3,))[at]:
                     pass_line(x_line(j))
                 if at == 3:
                     end_z(0)

time: 157 us -> 157 us (level)
  no operation moved by 1% of the time
where the time goes in v5:
time: 157 us
  Pallas kernels  156 us (99%)
    pallas_call x1, Pallas kernels, run_kernel(): pl.pallas_call(functools.partial(kernel, scattering), out_shape=tuple((ja...  153 us

profile of v5, /device:TPU:0, one launch (start us, length us, event | category | flops | bytes accessed | tf_op | source)
XLA Modules:
  0.0 156.6 jit_solution(1518734752815252547)
XLA Ops:
  0.6 152.9 %relay_layers.1 = (f32[2,256,768]{2,1,0:T(8,128)}, f32[48,2304]{1,0:T(8,128)}, f32[48,768]{1,0:T(8,128)}, f32[48,3072]{1,0:T(8,128)}, f32[192,768]{1,0:T(8,128)}, /*index=5*/f32[2,48]{1,0:T(2,128)}) custom-call(s32[2]{0:T(128)} %counts_ref.1, f32[2,768]{1,0:T(2,128)} %bitcast.15, bf16[2,256,768]{2,1,0:T(8,128)(2,1)} %acts_ref.1, ...), custom_call_target="tpu_custom_call" | custom-call | tf_op jit(solution)/shard_map/relay_layers/pallas_call | solution.py:833
  153.5 3.0 %hand_over.1 = (f32[2,256,768]{2,1,0:T(8,128)}, f32[48,2304]{1,0:T(8,128)}, f32[48,768]{1,0:T(8,128)}, f32[48,3072]{1,0:T(8,128)}, f32[192,768]{1,0:T(8,128)}, /*index=5*/f32[2,48]{1,0:T(2,128)}) custom-call(f32[2,256,768]{2,1,0:T(8,128)} %get-tuple-element.18.refs_0_, f32[48,2304]{1,0:T(8,128)} %get-tuple-element.19.refs_1_, ...), custom_call_target="tpu_custom_call" | custom-call | tf_op jit(solution)/shard_map/hand_over/pallas_call | solution.py:879
